TPU v7x, 32 devices: a whole 2x2x4 slice. The times are simulated.
32 devices in a mesh: scan: 16 (over z, y, x), mode: 2 (over core).
Axes of the slice: x: 2, y: 2, z: 4, core: 2. Of those that a mesh axis runs over, the one named last changes fastest.
Arguments:
- object_field: float32 [2, 640, 1152], P(None, 'scan'), may hold values from -4.5 to 4.5
- probe: float32 [8, 2, 512, 512], P('mode'), may hold values from -1.5 to 1.5
- amplitude: float32 [16, 512, 512], P('scan'), may hold values from 0.2 to 1.8
- pos_row: int32 [16], P('scan'), may hold values from 0 to 128, as said below
- pos_col: int32 [16], P('scan'), may hold values from 0 to 640, as said below
- strip_of: int32 [16], P('scan'), may hold values from 0 to 15, each once
Outputs:
- object_grad: float32 [2, 640, 1152], P(None, 'scan')
- probe_grad: float32 [8, 2, 512, 512], P('mode')
Inputs may be any that keep to these rules, and one draw needn't show every extreme that they name: Pattern p covers object rows pos_row[p] to pos_row[p] + 511; the smallest and the largest allowed value both occur. Pattern p covers object columns pos_col[p] to pos_col[p] + 511; the smallest and the largest allowed value both occur.
All inputs are finite; a program needn't handle non-finite values.
Results may differ from a plain program's by a relative error of at most 0.0055.
The roundings to bfloat16 on the way count: a program that leaves them out, or rounds other values in their place, can miss the bound.
Values may be sent and summed in bfloat16 or wider, within the bound.
A program may use at most 128 MiB of HBM per device.

v0:
```python
import math
import jax
import jax.numpy as jnp
from jax import lax
from jax.sharding import PartitionSpec as P


def dft_table(sign_factor, probe_size):
    positions = jnp.arange(probe_size, dtype=jnp.int32)
    products = positions[:, None] * positions[None, :] % probe_size
    angle_table = products.astype(jnp.float32) * (2.0 * math.pi / probe_size)
    norm_scale = 1.0 / math.sqrt(probe_size)
    cosine = jnp.cos(angle_table) * norm_scale
    sine_part = jnp.sin(angle_table) * (sign_factor * norm_scale)
    return jnp.stack([jnp.stack([cosine, sine_part]), jnp.stack([-sine_part, cosine])]).astype(
        jnp.bfloat16
    )


def transform(field_wave, matrix_table):
    half_wave = jnp.einsum(
        "oiab,pmibx->pmoax", matrix_table, field_wave, preferred_element_type=jnp.float32
    ).astype(jnp.bfloat16)
    return jnp.einsum(
        "pmiax,oixy->pmoay", half_wave, matrix_table, preferred_element_type=jnp.float32
    )


def shards(object_field, probe, amplitude, pos_row, pos_col, strip_of):
    probe_size = probe.shape[-1]
    strip_rows = object_field.shape[1]
    obj_cols = object_field.shape[2]
    pat_count = pos_row.shape[0]
    devices = lax.axis_size("scan")
    held_rows = devices * strip_rows
    all_strips, all_cols = (
        lax.all_gather(strip_of, "scan", axis=0, tiled=True),
        lax.all_gather(pos_col, "scan", axis=0, tiled=True),
    )
    device_ids = jnp.arange(devices, dtype=jnp.int32)
    owner_of = jnp.sum(
        jnp.where(all_strips[None, :] == device_ids[:, None], device_ids[None, :], 0), axis=1
    )
    inside_rows = jnp.tile(jnp.arange(strip_rows, dtype=jnp.int32), devices)
    held_of_window = jnp.repeat(owner_of, strip_rows) * strip_rows + inside_rows
    window_of_held = jnp.repeat(all_strips, strip_rows) * strip_rows + inside_rows

    def patch_rows(row_start):
        return lax.dynamic_slice_in_dim(held_of_window, row_start, probe_size)

    held_index = jax.vmap(patch_rows)(pos_row)
    object_half = object_field.astype(jnp.bfloat16)
    gathered = lax.all_gather(object_half, "scan", axis=1, tiled=True)

    def take_patch(rows_wanted, col_start):
        band_rows = jnp.take(gathered, rows_wanted, axis=1)
        return lax.dynamic_slice_in_dim(band_rows, col_start, probe_size, 2)

    patches = jax.vmap(take_patch)(held_index, pos_col)
    patch_wide = patches.astype(jnp.float32)
    patch_re = patch_wide[:, None, 0]
    patch_im = patch_wide[:, None, 1]
    probe_re = probe[:, 0]
    probe_im = probe[:, 1]
    exit_re = probe_re * patch_re - probe_im * patch_im
    exit_im = probe_re * patch_im + probe_im * patch_re
    exit_wave = jnp.stack([exit_re, exit_im], axis=2).astype(jnp.bfloat16)
    forward = dft_table(1.0, probe_size)
    inverse = dft_table(-1.0, probe_size)
    far_field = transform(exit_wave, forward)
    local_power = jnp.sum(
        far_field[:, :, 0] * far_field[:, :, 0] + far_field[:, :, 1] * far_field[:, :, 1], axis=1
    )
    intensity = lax.psum(local_power, "mode")
    scale_factor = 1.0 - amplitude / jnp.sqrt(jnp.maximum(intensity, 0.25))
    residual_wave = (far_field * scale_factor[:, None, None]).astype(jnp.bfloat16)
    back_wave = transform(residual_wave, inverse)
    back_re = back_wave[:, :, 0]
    back_im = back_wave[:, :, 1]
    grad_re = jnp.sum(probe_re * back_re + probe_im * back_im, axis=1)
    grad_im = jnp.sum(probe_re * back_im - probe_im * back_re, axis=1)
    patch_grad = jnp.stack([grad_re, grad_im], axis=1)
    term_re = jnp.sum(patch_re * back_re + patch_im * back_im, axis=0)
    term_im = jnp.sum(patch_re * back_im - patch_im * back_re, axis=0)
    probe_grad = lax.psum(jnp.stack([term_re, term_im], axis=1), "scan")
    patch_grad = lax.psum(patch_grad, "mode")

    def band_of(grad_piece, row_start):
        band_rows = jnp.zeros((2, held_rows, probe_size), jnp.float32)
        band_rows = lax.dynamic_update_slice_in_dim(band_rows, grad_piece, row_start, 1)
        return jnp.take(band_rows, window_of_held, axis=1)

    bands = jax.vmap(band_of)(patch_grad, pos_row)
    received = lax.all_to_all(bands, "scan", split_axis=2, concat_axis=0, tiled=True)

    def add_piece(slot_index, strip_total):
        col_start = all_cols[slot_index]
        current = lax.dynamic_slice_in_dim(strip_total, col_start, probe_size, 2)
        return lax.dynamic_update_slice_in_dim(
            strip_total, current + received[slot_index], col_start, 2
        )

    object_grad = lax.fori_loop(
        0, devices * pat_count, add_piece, jnp.zeros((2, strip_rows, obj_cols), jnp.float32)
    )
    return (object_grad, probe_grad)


def solution(mesh):
    return jax.shard_map(
        shards,
        mesh=mesh,
        in_specs=(
            P(None, "scan", None),
            P("mode", None, None, None),
            P("scan", None, None),
            P("scan"),
            P("scan"),
            P("scan"),
        ),
        out_specs=(P(None, "scan", None), P("mode", None, None, None)),
        check_vma=False,
    )
```

profile of v0, /device:TPU:0, one launch (start us, length us, event | category | flops | bytes accessed | tf_op | source)
XLA Modules:
  0.0 562.3 jit_solution(8527928719411964411)
XLA Ops:
  11.1 7.8 %fusion.57 = (f32[4,1,512,512]{3,2,1,0:T(8,128)}, f32[4,1,512,512]{3,2,1,0:T(8,128)}) fusion(f32[4,2,512,512]{3,2,1,0:T(8,128)} %param.11), kind=kLoop, calls=%fused_computation.103 | loop fusion | bytes 16777216 | tf_op jit(solution)/shard_map/slice | solution.py:63
  18.9 5.3 copy.123
  24.1 5.3 copy.122
  31.5 16.2 %all-reduce.3 = (s32[16]{0:T(128)S(1)}, s32[16]{0:T(128)S(1)}) all-reduce(s32[16]{0:T(128)S(1)} %dynamic-update-slice.5, s32[16]{0:T(128)S(1)} %dynamic-update-slice.6), channel_id=1, replica_groups=mesh['scan'=16,'mode'=2] {'scan'}, use_global_device_ids=true, to_apply=%add.1 | all-reduce | flops 32 | bytes 256
  48.1 4.0 multiply_convert_fusion.3
  52.1 4.4 multiply_convert_fusion.1
  56.5 4.0 negate_convert_fusion
  62.7 17.7 %all-gather.2.cloned.1.call-done = bf16[2,640,1152]{2,0,1:T(2,128)(2,1)} async-done(((bf16[2,40,1152]{2,0,1:T(2,128)(2,1)}), bf16[2,640,1152]{2,0,1:T(2,128)(2,1)}) %all-gather.2.cloned.1.call-update) | async-done | bytes 2949136 | tf_op jit(solution)/shard_map/all_gather | solution.py:53
  80.4 28.6 %gather_fusion = bf16[512,2,1152]{2,1,0:T(2,128)(2,1)S(1)} fusion(bf16[2,640,1152]{2,0,1:T(2,128)(2,1)} %all-gather.2.cloned.1.call-done, s32[1024]{0:T(1024)S(1)} %pad_clamp_fusion.1), kind=kCustom, calls=%fused_computation | custom fusion | bytes 4720640 | tf_op jit(solution)/shard_map/vmap(jit(_take))/gather | solution.py:56
  108.9 3.7 fusion.40
  117.2 6.4 %fusion.23 = bf16[4,1,512,512]{2,3,1,0:T(8,128)(2,1)} fusion(f32[4,1,512,512]{2,3,0,1:T(8,128)} %copy.123, f32[4,1,512,512]{2,3,0,1:T(8,128)} %copy.122, f32[512,512]{0,1:T(8,128)S(1)} %bitcast.213, f32[512,512]{0,1:T(8,128)S(1)} %bitcast.216), kind=kLoop, calls=%fused_computation.42 | loop fusion | flops 4194304 | bytes 12582912 | tf_op jit(solution)/shard_map/convert.1
  123.6 2.8 fusion.31
  126.4 15.1 %fusion.27 = f32[1,4,2,512,512]{3,4,1,2,0:T(8,128)} fusion(bf16[1,2,512,512]{3,2,1,0:T(8,128)(2,1)S(1)} %copy-done.3, bf16[1,2,512,512]{3,2,1,0:T(8,128)(2,1)} %get-tuple-element.158, bf16[4,1,512,512]{2,3,1,0:T(8,128)(2,1)} %fusion.23, bf16[4,1,512,512]{2,3,1,0:T(8,128)(2,1)} %fusion.31), kind=kOutput, calls=%fused_computation.44 | convolution fusion | flops 8608808960 | bytes 14680064 | tf_op jit(solution)/shard_map/pmiax,oixy->pmoay/dot_general | solution.py:24
  141.5 6.1 %fusion.12 = f32[512,512]{0,1:T(8,128)} fusion(f32[1,4,2,512,512]{3,4,1,2,0:T(8,128)} %fusion.27), kind=kLoop, calls=%fused_computation.20 | loop fusion | flops 3932160 | bytes 9437184 | tf_op jit(solution)/shard_map/reduce_sum | solution.py:71
  149.3 17.2 %all-reduce.8.cloned.1.call-done = f32[1,512,512]{1,2,0:T(8,128)} async-done(((f32[1,512,512]{1,2,0:T(8,128)}), f32[1,512,512]{1,2,0:T(8,128)}) %all-reduce.8.cloned.1.call-update) | async-done | bytes 1048592 | tf_op jit(solution)/shard_map/psum | solution.py:74
  166.5 2.5 subtract_bitcast_fusion
  168.9 15.9 %fusion.24 = f32[1,4,2,512,512]{3,4,1,2,0:T(8,128)} fusion(bf16[1,2,512,512]{3,2,1,0:T(8,128)(2,1)} %get-tuple-element.159, bf16[1,2,512,512]{3,2,1,0:T(8,128)(2,1)} %get-tuple-element.156, f32[1,4,2,512,512]{3,4,1,2,0:T(8,128)} %fusion.27, f32[512,512]{0,1:T(8,128)} %subtract_bitcast_fusion), kind=kOutput, calls=%fused_computation.43 | convolution fusion | flops 8602517504 | bytes 19922944 | tf_op jit(solution)/shard_map/pmiax,oixy->pmoay/dot_general | solution.py:24
  184.8 8.1 %fusion.17 = (f32[512,512]{0,1:T(8,128)S(1)}, f32[512,512]{0,1:T(8,128)}) fusion(f32[4,1,512,512]{2,3,0,1:T(8,128)} %copy.123, f32[4,1,512,512]{2,3,0,1:T(8,128)} %copy.122, f32[1,4,2,512,512]{3,4,1,2,0:T(8,128)} %fusion.24), kind=kLoop, calls=%fused_computation.33 | loop fusion | flops 7864320 | bytes 18874368 | tf_op jit(solution)/shard_map/reduce_sum | solution.py:80
  192.9 3.6 copy.120
  198.5 4.8 pad_maximum_fusion.3
  203.5 4.8 fusion.3
  208.3 4.7 pad_maximum_fusion
  214.4 2.7 and_reduce_fusion
  217.1 8.7 %all-reduce.10.cloned.1.call-done = f32[1,2,512,512]{3,1,2,0:T(2,128)} async-done(((f32[1,2,512,512]{3,1,2,0:T(2,128)}), f32[1,2,512,512]{3,1,2,0:T(2,128)}) %all-reduce.10.cloned.1.call-update) | async-done | bytes 2097168 | tf_op jit(solution)/shard_map/psum | solution.py:86
  226.5 3.9 bitcast_dynamic-update-slice_fusion
  230.5 5.5 gather_fusion.1
  236.0 5.3 fusion.30
  241.3 6.8 %all-to-all-start = ((f32[1,2,640,512]{3,1,0,2:T(2,128)}), f32[1,2,640,512]{3,1,0,2:T(2,128)S(1)}, u32[]{:S(2)}, u32[]{:S(2)}) async-start(f32[1,2,640,512]{3,1,0,2:T(2,128)} %fusion.30), calls=%async_computation | async-start | bytes 5242880 | tf_op jit(solution)/shard_map/all_to_all | solution.py:94
  248.1 89.7 %all-to-all-done = f32[1,2,640,512]{3,1,0,2:T(2,128)S(1)} async-done(((f32[1,2,640,512]{3,1,0,2:T(2,128)}), f32[1,2,640,512]{3,1,0,2:T(2,128)S(1)}, u32[]{:S(2)}, u32[]{:S(2)}) %all-to-all-start) | async-done | bytes 2621472 | tf_op jit(solution)/shard_map/all_to_all | solution.py:94
  339.9 72.8 %while.16 = (s32[]{:T(128)}, f32[2,40,1152]{2,1,0:T(8,128)S(1)}, s32[16]{0:T(128)S(1)}, f32[16,2,40,512]{3,2,0,1:T(8,128)}, s32[]{:T(128)}, /*index=5*/s32[]{:T(128)}, s32[]{:T(128)}) while((s32[]{:T(128)}, f32[2,40,1152]{2,1,0:T(8,128)S(1)}, s32[16]{0:T(128)S(1)}, f32[16,2,40,512]{3,2,0,1:T(8,128)}, s32[]{:T(128)}, /*index=5*/s32[]{:T(128)}, ...), condition=%wide.region_8.9_spmd, body=%wide.region_7.8_spmd.sunk | while | flops 40965 | bytes 819343 | solution.py:103
  412.7 133.0 %all-reduce.12.cloned.1.call-done = f32[4,2,512,512]{2,3,1,0:T(8,128)} async-done(((f32[4,2,512,512]{2,3,1,0:T(8,128)}), f32[4,2,512,512]{2,3,1,0:T(8,128)}) %all-reduce.12.cloned.1.call-update) | async-done | bytes 8388624 | tf_op jit(solution)/shard_map/psum | solution.py:85
  545.7 9.9 %copy.98 = f32[4,2,512,512]{3,2,1,0:T(8,128)} copy(f32[4,2,512,512]{2,3,1,0:T(8,128)} %all-reduce.12.cloned.1.call-done) | data formatting | bytes 16777216
  (101 shorter events, 62.1 us)
Async XLA Ops:
  7.2 73.2 %all-gather.2.cloned.1.call-start = ((), (), s32[]{:S(2)}) async-start(), calls=%async_computation.1 | async-start | bytes 3133440 | tf_op jit(solution)/shard_map/all_gather | solution.py:53
  9.1 157.4 %all-reduce.8.cloned.1.call-start = ((), (), s32[]{:S(2)}) async-start(), calls=%async_computation.2 | async-start | bytes 2097152 | tf_op jit(solution)/shard_map/psum | solution.py:74
  24.1 5.3 copy-start.6
  117.1 6.4 %copy-start = (f32[4,1,512,512]{2,3,0,1:T(8,128)S(1)}, f32[4,1,512,512]{2,3,0,1:T(8,128)}, u32[]{:S(2)}) copy-start(f32[4,1,512,512]{2,3,0,1:T(8,128)} %copy.123) | copy-start | bytes 12582916
  117.2 6.4 %copy-start.1 = (f32[4,1,512,512]{2,3,0,1:T(8,128)S(1)}, f32[4,1,512,512]{2,3,0,1:T(8,128)}, u32[]{:S(2)}) copy-start(f32[4,1,512,512]{2,3,0,1:T(8,128)} %copy.122) | copy-start | bytes 12582916
  123.6 2.8 copy-start.3
  147.6 78.2 %all-reduce.10.cloned.1.call-start = ((), (), s32[]{:S(2)}) async-start(), calls=%async_computation.3 | async-start | bytes 4194304 | tf_op jit(solution)/shard_map/psum | solution.py:86
  203.3 342.4 %all-reduce.12.cloned.1.call-start = ((), (), s32[]{:S(2)}) async-start(), calls=%async_computation.4 | async-start | bytes 16777216 | tf_op jit(solution)/shard_map/psum | solution.py:85
  213.0 0.7 copy-start.5
  213.0 1.4 copy-start.4
  241.3 96.5 %all-to-all-start = ((f32[1,2,640,512]{3,1,0,2:T(2,128)}), f32[1,2,640,512]{3,1,0,2:T(2,128)S(1)}, u32[]{:S(2)}, u32[]{:S(2)}) async-start(f32[1,2,640,512]{3,1,0,2:T(2,128)} %fusion.30), calls=%async_computation | async-start | bytes 5242880 | tf_op jit(solution)/shard_map/all_to_all | solution.py:94
  412.7 142.9 %copy-start.2 = (f32[2,40,1152]{2,1,0:T(8,128)}, f32[2,40,1152]{2,1,0:T(8,128)S(1)}, u32[]{:S(2)}) copy-start(f32[2,40,1152]{2,1,0:T(8,128)S(1)} %get-tuple-element.134) | copy-start | bytes 1105924
Sparse Core Ops, SparseCore 0:
  11.4 68.9 all-gather.1
  147.8 18.6 all-reduce.7
  203.4 22.3 all-reduce.9
  232.3 313.3 all-reduce.11
where the time goes:
time: 569 us; the launch traced here: 562 us
  waiting for transfers between devices  266 us (47%)
  local copies, waits for them, and re-layouts  108 us (19%)
  other arithmetic  87.6 us (15%)
  matrix products  31 us (5%)
  loops' own time  29.7 us (5%)
  blocking collectives  16.2 us (3%)
  between operations  16.1 us (3%)
  starting transfers between devices  7.12 us (1%)
    psum x1, waiting for transfers between devices, shards(): probe_grad = lax.psum(jnp.stack([term_re, term_im], axis=1), 'scan')  133 us
    all_to_all x1, waiting for transfers between devices, shards(): lax.all_to_all(bands, 'scan', split_axis=2, concat_axis=0, tiled=True)  89.7 us
    dot_general x2, matrix products, transform(): jnp.einsum('pmiax,oixy->pmoay', half_wave, matrix_table, preferred_elemen...  31 us
    another operation x1, loops' own time, shards(): lax.fori_loop(0, devices * pat_count, add_piece, jnp.zeros((2, strip_rows...  29.7 us
    gather x1, local copies, waits for them, and re-layouts, take_patch(): band_rows = jnp.take(gathered, rows_wanted, axis=1)  28.6 us
    unnamed x24, local copies, waits for them, and re-layouts  26.3 us
    another operation x6, other arithmetic  24.3 us
    all_gather x1, waiting for transfers between devices, shards(): gathered = lax.all_gather(object_half, 'scan', axis=1, tiled=True)  17.7 us
  transfers between devices with their start and end apart: 5, of which 5 were waited for; matrix products, arithmetic and copies ran while one was open for 20% of the time, Pallas kernels for 0%

commit v1 on v0

--- a/solution.py
+++ b/solution.py
@@ -91,7 +91,10 @@
         return jnp.take(band_rows, window_of_held, axis=1)
 
     bands = jax.vmap(band_of)(patch_grad, pos_row)
-    received = lax.all_to_all(bands, "scan", split_axis=2, concat_axis=0, tiled=True)
+    received = jnp.concatenate(
+        lax.all_to_all(jnp.stack(jnp.split(bands, lax.axis_size("scan"), axis=2)), "scan", 0, 0),
+        axis=0,
+    )
 
     def add_piece(slot_index, strip_total):
         col_start = all_cols[slot_index]

time: 569 us -> 595 us (1.046)
  local copies, waits for them, and re-layouts: 108 us -> 136 us
  other arithmetic: 87.6 us -> 70.1 us
  waiting for transfers between devices: 266 us -> 281 us
    psum x1, waiting for transfers between devices: 133 us -> 151 us  [shards(): probe_grad = lax.psum(jnp.stack([term_re, term_im], axis=1), 'scan')]
    dynamic_slice x0 -> x16, local copies, waits for them, and re-layouts: none -> 15 us  [add_piece(): received[slot_index]]
    add x16, other arithmetic: 16.6 us -> 1.83 us  [add_piece(): current + received[slot_index]]
    all_to_all x1, waiting for transfers between devices: 89.7 us -> 76 us  [shards(): lax.all_to_all(jnp.stack(jnp.split(bands, lax.axis_size('scan'), axis=2))...]
    psum x1, waiting for transfers between devices: 8.7 us -> 18.9 us  [shards(): patch_grad = lax.psum(patch_grad, 'mode')]
    unnamed x24 -> x41, local copies, waits for them, and re-layouts: 26.3 us -> 36 us
  transfers between devices with their start and end apart: 5 -> 5, of which waited for: 5 -> 5; matrix products, arithmetic and copies ran while one was open for 20% -> 16% of each run, Pallas kernels for 0% -> 0%
where the time goes in v1:
time: 595 us; the launch traced here: 588 us
  waiting for transfers between devices  281 us (47%)
  local copies, waits for them, and re-layouts  136 us (23%)
  other arithmetic  70.1 us (12%)
  matrix products  31 us (5%)
  loops' own time  30.4 us (5%)
  blocking collectives  16.2 us (3%)
  between operations  16.2 us (3%)
  starting transfers between devices  7 us (1%)
    psum x1, waiting for transfers between devices, shards(): probe_grad = lax.psum(jnp.stack([term_re, term_im], axis=1), 'scan')  151 us
    all_to_all x1, waiting for transfers between devices, shards(): lax.all_to_all(jnp.stack(jnp.split(bands, lax.axis_size('scan'), axis=2))...  76 us
    unnamed x41, local copies, waits for them, and re-layouts  36 us
    dot_general x2, matrix products, transform(): jnp.einsum('pmiax,oixy->pmoay', half_wave, matrix_table, preferred_elemen...  31 us
    another operation x1, loops' own time, shards(): lax.fori_loop(0, devices * pat_count, add_piece, jnp.zeros((2, strip_rows...  30.4 us
    gather x1, local copies, waits for them, and re-layouts, take_patch(): band_rows = jnp.take(gathered, rows_wanted, axis=1)  28.6 us
    another operation x6, other arithmetic  24.2 us
    psum x1, waiting for transfers between devices, shards(): patch_grad = lax.psum(patch_grad, 'mode')  18.9 us
  transfers between devices with their start and end apart: 5, of which 5 were waited for; matrix products, arithmetic and copies ran while one was open for 16% of the time, Pallas kernels for 0%

profile of v1, /device:TPU:0, one launch (start us, length us, event | category | flops | bytes accessed | tf_op | source)
XLA Modules:
  0.0 587.9 jit_solution(14502161718461372007)
XLA Ops:
  11.1 7.8 %fusion.73 = (f32[4,1,512,512]{3,2,1,0:T(8,128)}, f32[4,1,512,512]{3,2,1,0:T(8,128)}) fusion(f32[4,2,512,512]{3,2,1,0:T(8,128)} %param.11), kind=kLoop, calls=%fused_computation.136 | loop fusion | bytes 16777216 | tf_op jit(solution)/shard_map/slice | solution.py:63
  18.9 5.3 copy.133
  24.2 5.3 copy.132
  31.5 16.2 %all-reduce.3 = (s32[16]{0:T(128)S(1)}, s32[16]{0:T(128)S(1)}) all-reduce(s32[16]{0:T(128)S(1)} %dynamic-update-slice.5, s32[16]{0:T(128)S(1)} %dynamic-update-slice.6), channel_id=1, replica_groups=mesh['scan'=16,'mode'=2] {'scan'}, use_global_device_ids=true, to_apply=%add.1 | all-reduce | flops 32 | bytes 256
  48.1 4.0 multiply_convert_fusion.3
  52.1 4.4 multiply_convert_fusion.1
  56.5 4.0 negate_convert_fusion
  62.7 17.6 %all-gather.2.cloned.1.call-done = bf16[2,640,1152]{2,0,1:T(2,128)(2,1)} async-done(((bf16[2,40,1152]{2,0,1:T(2,128)(2,1)}), bf16[2,640,1152]{2,0,1:T(2,128)(2,1)}) %all-gather.2.cloned.1.call-update) | async-done | bytes 2949136 | tf_op jit(solution)/shard_map/all_gather | solution.py:53
  80.3 28.6 %gather_fusion = bf16[512,2,1152]{2,1,0:T(2,128)(2,1)S(1)} fusion(bf16[2,640,1152]{2,0,1:T(2,128)(2,1)} %all-gather.2.cloned.1.call-done, s32[1024]{0:T(1024)S(1)} %pad_clamp_fusion.1), kind=kCustom, calls=%fused_computation | custom fusion | bytes 4720640 | tf_op jit(solution)/shard_map/vmap(jit(_take))/gather | solution.py:56
  108.9 3.7 fusion.40
  117.3 6.4 %fusion.24 = bf16[4,1,512,512]{2,3,1,0:T(8,128)(2,1)} fusion(f32[4,1,512,512]{2,3,0,1:T(8,128)} %copy.133, f32[4,1,512,512]{2,3,0,1:T(8,128)} %copy.132, f32[512,512]{0,1:T(8,128)S(1)} %bitcast.269, f32[512,512]{0,1:T(8,128)S(1)} %bitcast.272), kind=kLoop, calls=%fused_computation.44 | loop fusion | flops 4194304 | bytes 12582912 | tf_op jit(solution)/shard_map/convert.1
  123.8 2.8 fusion.31
  126.6 15.1 %fusion.28 = f32[1,4,2,512,512]{3,4,1,2,0:T(8,128)} fusion(bf16[1,2,512,512]{3,2,1,0:T(8,128)(2,1)S(1)} %copy-done.4, bf16[1,2,512,512]{3,2,1,0:T(8,128)(2,1)} %get-tuple-element.158, bf16[4,1,512,512]{2,3,1,0:T(8,128)(2,1)} %fusion.24, bf16[4,1,512,512]{2,3,1,0:T(8,128)(2,1)} %fusion.31), kind=kOutput, calls=%fused_computation.46 | convolution fusion | flops 8608808960 | bytes 14680064 | tf_op jit(solution)/shard_map/pmiax,oixy->pmoay/dot_general | solution.py:24
  141.7 5.8 fusion.13
  149.2 17.2 %all-reduce.8.cloned.1.call-done = f32[1,512,512]{1,2,0:T(8,128)} async-done(((f32[1,512,512]{1,2,0:T(8,128)}), f32[1,512,512]{1,2,0:T(8,128)}) %all-reduce.8.cloned.1.call-update) | async-done | bytes 1048592 | tf_op jit(solution)/shard_map/psum | solution.py:74
  166.4 2.4 subtract_bitcast_fusion
  168.9 15.9 %fusion.25 = f32[1,4,2,512,512]{3,4,1,2,0:T(8,128)} fusion(bf16[1,2,512,512]{3,2,1,0:T(8,128)(2,1)} %get-tuple-element.159, bf16[1,2,512,512]{3,2,1,0:T(8,128)(2,1)} %get-tuple-element.156, f32[1,4,2,512,512]{3,4,1,2,0:T(8,128)} %fusion.28, f32[512,512]{0,1:T(8,128)} %subtract_bitcast_fusion), kind=kOutput, calls=%fused_computation.45 | convolution fusion | flops 8602517504 | bytes 19922944 | tf_op jit(solution)/shard_map/pmiax,oixy->pmoay/dot_general | solution.py:24
  184.7 8.1 %fusion.18 = (f32[512,512]{0,1:T(8,128)S(1)}, f32[512,512]{0,1:T(8,128)}) fusion(f32[4,1,512,512]{2,3,0,1:T(8,128)} %copy.133, f32[4,1,512,512]{2,3,0,1:T(8,128)} %copy.132, f32[1,4,2,512,512]{3,4,1,2,0:T(8,128)} %fusion.25), kind=kLoop, calls=%fused_computation.35 | loop fusion | flops 7864320 | bytes 18874368 | tf_op jit(solution)/shard_map/reduce_sum | solution.py:80
  192.9 3.6 copy.130
  198.4 4.8 pad_maximum_fusion.3
  204.2 2.6 and_reduce_fusion
  206.8 18.9 %all-reduce.10.cloned.1.call-done = f32[1,2,512,512]{3,1,2,0:T(2,128)} async-done(((f32[1,2,512,512]{3,1,2,0:T(2,128)}), f32[1,2,512,512]{3,1,2,0:T(2,128)}) %all-reduce.10.cloned.1.call-update) | async-done | bytes 2097168 | tf_op jit(solution)/shard_map/psum | solution.py:86
  227.9 3.4 bitcast_dynamic-update-slice_fusion
  231.4 8.8 %gather_fusion.1 = f32[640,2,512]{2,1,0:T(2,128)} fusion(f32[2,640,512]{2,0,1:T(2,128)} %bitcast_dynamic-update-slice_fusion, s32[1024]{0:T(1024)S(1)} %pad_clamp_fusion), kind=kCustom, calls=%fused_computation.1 | custom fusion | bytes 5245440 | tf_op jit(solution)/shard_map/vmap(jit(_take))/gather | solution.py:91
  240.2 3.9 bitcast_select_fusion
  254.9 6.8 %all-to-all-start = ((f32[16,1,2,40,512]{4,2,3,1,0:T(2,128)}), f32[16,1,2,40,512]{4,2,3,1,0:T(2,128)}, u32[]{:S(2)}, u32[]{:S(2)}) async-start(f32[16,1,2,40,512]{4,2,3,1,0:T(2,128)} %fusion.52), calls=%async_computation | async-start | bytes 5242880 | tf_op jit(solution)/shard_map/all_to_all | solution.py:95
  261.7 4.8 fusion.4
  266.5 4.4 pad_maximum_fusion
  271.0 76.0 %all-to-all-done = f32[16,1,2,40,512]{4,2,3,1,0:T(2,128)} async-done(((f32[16,1,2,40,512]{4,2,3,1,0:T(2,128)}), f32[16,1,2,40,512]{4,2,3,1,0:T(2,128)}, u32[]{:S(2)}, u32[]{:S(2)}) %all-to-all-start) | async-done | bytes 2621472 | tf_op jit(solution)/shard_map/all_to_all | solution.py:95
  347.0 73.5 %while.16 = (s32[]{:T(128)}, f32[2,40,1152]{2,1,0:T(8,128)S(1)}, s32[16]{0:T(128)S(1)}, f32[16,2,40,512]{3,1,2,0:T(2,128)}, s32[]{:T(128)}, /*index=5*/s32[]{:T(128)}, s32[]{:T(128)}) while((s32[]{:T(128)}, f32[2,40,1152]{2,1,0:T(8,128)S(1)}, s32[16]{0:T(128)S(1)}, f32[16,2,40,512]{3,1,2,0:T(2,128)}, s32[]{:T(128)}, /*index=5*/s32[]{:T(128)}, ...), condition=%wide.region_8.9_spmd, body=%wide.region_7.8_spmd.sunk | while | flops 40965 | bytes 1147023 | solution.py:106
  420.5 150.8 %all-reduce.12.cloned.1.call-done = f32[4,2,512,512]{2,3,1,0:T(8,128)} async-done(((f32[4,2,512,512]{2,3,1,0:T(8,128)}), f32[4,2,512,512]{2,3,1,0:T(8,128)}) %all-reduce.12.cloned.1.call-update) | async-done | bytes 8388624 | tf_op jit(solution)/shard_map/psum | solution.py:85
  571.3 9.9 %copy.108 = f32[4,2,512,512]{3,2,1,0:T(8,128)} copy(f32[4,2,512,512]{2,3,1,0:T(8,128)} %all-reduce.12.cloned.1.call-done) | data formatting | bytes 16777216
  (134 shorter events, 71.8 us)
Async XLA Ops:
  7.2 73.2 %all-gather.2.cloned.1.call-start = ((), (), s32[]{:S(2)}) async-start(), calls=%async_computation.1 | async-start | bytes 3133440 | tf_op jit(solution)/shard_map/all_gather | solution.py:53
  9.1 157.3 %all-reduce.8.cloned.1.call-start = ((), (), s32[]{:S(2)}) async-start(), calls=%async_computation.2 | async-start | bytes 2097152 | tf_op jit(solution)/shard_map/psum | solution.py:74
  24.2 5.3 copy-start.7
  117.3 6.4 %copy-start = (f32[4,1,512,512]{2,3,0,1:T(8,128)S(1)}, f32[4,1,512,512]{2,3,0,1:T(8,128)}, u32[]{:S(2)}) copy-start(f32[4,1,512,512]{2,3,0,1:T(8,128)} %copy.133) | copy-start | bytes 12582916
  117.3 6.4 %copy-start.1 = (f32[4,1,512,512]{2,3,0,1:T(8,128)S(1)}, f32[4,1,512,512]{2,3,0,1:T(8,128)}, u32[]{:S(2)}) copy-start(f32[4,1,512,512]{2,3,0,1:T(8,128)} %copy.132) | copy-start | bytes 12582916
  123.8 2.8 copy-start.4
  147.6 78.2 %all-reduce.10.cloned.1.call-start = ((), (), s32[]{:S(2)}) async-start(), calls=%async_computation.3 | async-start | bytes 4194304 | tf_op jit(solution)/shard_map/psum | solution.py:86
  198.4 5.1 copy-start.6
  198.4 5.8 copy-start.5
  225.8 2.2 copy-start.3
  254.9 92.2 %all-to-all-start = ((f32[16,1,2,40,512]{4,2,3,1,0:T(2,128)}), f32[16,1,2,40,512]{4,2,3,1,0:T(2,128)}, u32[]{:S(2)}, u32[]{:S(2)}) async-start(f32[16,1,2,40,512]{4,2,3,1,0:T(2,128)} %fusion.52), calls=%async_computation | async-start | bytes 5242880 | tf_op jit(solution)/shard_map/all_to_all | solution.py:95
  261.7 309.6 %all-reduce.12.cloned.1.call-start = ((), (), s32[]{:S(2)}) async-start(), calls=%async_computation.4 | async-start | bytes 16777216 | tf_op jit(solution)/shard_map/psum | solution.py:85
  420.5 160.7 %copy-start.2 = (f32[2,40,1152]{2,1,0:T(8,128)}, f32[2,40,1152]{2,1,0:T(8,128)S(1)}, u32[]{:S(2)}) copy-start(f32[2,40,1152]{2,1,0:T(8,128)S(1)} %get-tuple-element.134) | copy-start | bytes 1105924
Sparse Core Ops, SparseCore 0:
  11.4 68.9 all-gather.1
  147.7 18.6 all-reduce.7
  203.3 22.3 all-reduce.9
  271.1 300.1 all-reduce.11
